TPU v7x, 32 devices: a whole 2x2x4 slice. The times are simulated.
32 devices in a mesh: box: 8 (over z, core), angle: 4 (over y, x).
Axes of the slice: x: 2, y: 2, z: 4, core: 2. Of those that a mesh axis runs over, the one named last changes fastest.
Arguments:
- coefficients: bfloat16 [2, 625, 49152], P(None, None, ('box', 'angle')), may hold values from -6 to 6
- plane_map: bfloat16 [2, 625, 2048], P(None, None, 'angle'), may hold values from -0.15625 to 0.15625
- leaf_parent: int32 [49152], P('box'), may hold values from -1 to 768, as said below
- leaf_octant: int32 [49152], P('box'), may hold values from 0 to 7, as said below
- box_parent: int32 [6144], P('box'), may hold values from -1 to 96, as said below
- box_octant: int32 [6144], P('box'), may hold values from 0 to 7, as said below
- interp_one: float32 [4, 4096], P(None, 'angle'), may hold values from 0.05 to 0.6
- phase_one: float32 [8, 4096], P(None, 'angle'), may hold values from -3.140625 to 3.140625
- interp_two: float32 [4, 8192], P(None, 'angle'), may hold values from 0.05 to 0.6
- phase_two: float32 [8, 8192], P(None, 'angle'), may hold values from -3.140625 to 3.140625
Outputs:
- signature_one: float32 [6144, 2, 4096], P('box', None, 'angle')
- signature_two: float32 [768, 2, 8192], P('box', None, 'angle')
Inputs may be any that keep to these rules, and one draw needn't show every extreme that they name: `leaf_parent`: within each block of 6144 leaf slots: the slots with -1 come first, then live slots whose values never fall and name every slot from 0 to the block's live level-1 count minus 1, then slots with 768. Counting its children in both blocks, each level-1 box has 4 to 7 children. In every block but the last, the last live level-1 box has children in the next block, which hold that block's -1 slots; the first block has no -1 slot. A level-1 slot is named by some leaf exactly when its box_parent is not 96. `leaf_octant`: the children of one parent have distinct octants, rising along the slots; empty slots hold 0. `box_parent`: within each block of 768 level-1 slots: the slots with -1 come first, then live slots whose values never fall and name every slot from 0 to the block's level-2 count minus 1, then slots with 96. Counting its children in both blocks, each level-2 box has 4 to 7 children. In every block but the last, the last live level-2 box has children in the next block, which hold that block's -1 slots; the first block has no -1 slot. Some block uses all 96 level-2 slots. `box_octant`: the children of one parent have distinct octants, rising along the slots; empty slots hold 0.
All inputs are finite; a program needn't handle non-finite values.
Results may differ from a plain program's by a relative error of at most 0.0029.
Values may be sent and summed in bfloat16 or wider, within the bound.
A program may use at most 256 MiB of HBM per device.

v0:
```python
import jax
import jax.numpy as jnp
from jax import lax
from jax.sharding import PartitionSpec as P


def padded_2(cells, sides, width):
    for axis, dim in sides:
        count = lax.axis_size(axis)
        head = lax.slice_in_dim(cells, 0, width, axis=dim)
        tail = lax.slice_in_dim(cells, cells.shape[dim] - width, cells.shape[dim], axis=dim)
        cells = jnp.concatenate(
            [
                lax.ppermute(tail, axis, [(i, (i + 1) % count) for i in range(count)]),
                cells,
                lax.ppermute(head, axis, [((i + 1) % count, i) for i in range(count)]),
            ],
            axis=dim,
        )
    return cells


def passed_along(array, axis, by):
    peers = lax.axis_size(axis)
    pairs = [(i, i + by) for i in range(peers) if 0 <= i + by < peers]
    return lax.ppermute(array, axis, pairs)


def real_form(block):
    real_part = block[0]
    imag_part = block[1]
    upper = jnp.concatenate([real_part, imag_part], axis=1)
    lower = jnp.concatenate([-imag_part, real_part], axis=1)
    return jnp.concatenate([upper, lower], axis=0)


def leaf_product(coef_block, weights):
    count = coef_block.shape[2]
    width = weights.shape[1] // 2
    flat = coef_block.reshape(coef_block.shape[0] * coef_block.shape[1], count)
    product = lax.dot_general(
        flat, weights, (((0,), (0,)), ((), ())), preferred_element_type=jnp.float32
    )
    return product.reshape(count, 2, width).astype(jnp.bfloat16)


def octant_rows(octant, table):
    selector = (octant[:, None] == jnp.arange(8, dtype=jnp.int32)[None, :]).astype(jnp.float32)
    return jnp.dot(selector, table, precision=lax.Precision.HIGHEST)


def upsample_shift(padded, weights, octant, cosine, sine):
    width = padded.shape[-1] - 4
    even_weights = weights[:, 0::2]
    odd_weights = weights[:, 1::2]
    even_sum = jnp.zeros(padded.shape[:-1] + (width,), jnp.float32)
    odd_sum = jnp.zeros(padded.shape[:-1] + (width,), jnp.float32)
    for tap_index in range(4):
        window = padded[..., 1 + tap_index : 1 + tap_index + width].astype(jnp.float32)
        even_sum = even_sum + even_weights[tap_index] * window
        odd_sum = odd_sum + odd_weights[tap_index] * window
    total = jnp.stack([even_sum, odd_sum], axis=-1).reshape(padded.shape[:-1] + (2 * width,))
    cos_rows = octant_rows(octant, cosine)
    sin_rows = octant_rows(octant, sine)
    real_part = total[:, 0]
    imag_part = total[:, 1]
    return jnp.stack(
        [real_part * cos_rows - imag_part * sin_rows, real_part * sin_rows + imag_part * cos_rows],
        axis=1,
    )


def slot_sums(contrib, target, count):
    rows = contrib.shape[0]
    selector = (jnp.arange(count, dtype=jnp.int32)[:, None] == target[None, :]).astype(jnp.float32)
    flat = contrib.reshape(rows, -1)
    summed = jnp.dot(selector, flat, precision=lax.Precision.HIGHEST)
    return summed.reshape((count,) + contrib.shape[1:])


def attach_last(owned, incoming, last_slot):
    slot_ids = jnp.arange(owned.shape[0], dtype=jnp.int32)
    selector = (slot_ids == last_slot).astype(jnp.float32)
    return owned + selector[:, None, None] * incoming[None]


def body(
    coefficients,
    plane_map,
    leaf_parent,
    leaf_octant,
    box_parent,
    box_octant,
    interp_one,
    phase_one,
    interp_two,
    phase_two,
):
    slots_one = box_parent.shape[0]
    slots_two = slots_one // 8
    weights = real_form(plane_map)
    leaves = leaf_product(lax.all_gather(coefficients, "angle", axis=2, tiled=True), weights)
    padded = padded_2(leaves, (("angle", 2),), 2)
    target = jnp.where(leaf_parent < 0, slots_one + 1, leaf_parent)
    contrib_one = upsample_shift(
        padded, interp_one, leaf_octant, jnp.cos(phase_one), jnp.sin(phase_one)
    )
    sums_one = slot_sums(contrib_one, target, slots_one + 2)
    incoming = passed_along(sums_one[slots_one + 1], "box", -1)
    live_count = jnp.sum((box_parent != slots_two).astype(jnp.int32))
    signature_one = attach_last(sums_one[:slots_one], incoming, live_count - 1)
    padded_one = padded_2(signature_one, (("angle", 2),), 2)
    contrib_two = upsample_shift(
        padded_one, interp_two, box_octant, jnp.cos(phase_two), jnp.sin(phase_two)
    )
    target_two = jnp.where(box_parent < 0, slots_two + 1, box_parent)
    sums_two = slot_sums(contrib_two, target_two, slots_two + 2)
    incoming_two = passed_along(sums_two[slots_two + 1], "box", -1)
    last_two = jnp.max(jnp.where(box_parent < slots_two, box_parent, -1))
    signature_two = attach_last(sums_two[:slots_two], incoming_two, last_two)
    return (signature_one, signature_two)


def solution(mesh):
    in_specs = (
        P(None, None, ("box", "angle")),
        P(None, None, "angle"),
        P("box"),
        P("box"),
        P("box"),
        P("box"),
        P(None, "angle"),
        P(None, "angle"),
        P(None, "angle"),
        P(None, "angle"),
    )
    out_specs = (P("box", None, "angle"), P("box", None, "angle"))
    return jax.shard_map(body, mesh=mesh, in_specs=in_specs, out_specs=out_specs, check_vma=False)
```

profile of v0, /device:TPU:9, one launch (start us, length us, event | category | flops | bytes accessed | tf_op | source)
XLA Modules:
  0.0 764.7 jit_solution(12456914636370468835)
XLA Ops:
  7.2 0.0 copy-start.13
  7.2 0.0 copy-start.4
  7.2 0.0 copy-start.6
  7.2 0.0 all-gather.2.cloned.1.call-start
  7.3 0.7 all-gather.2.cloned.1.call-update
  7.9 1.1 slice.134
  9.0 1.1 slice.146
  10.1 4.1 fusion.44
  14.2 0.2 copy.51
  14.3 1.4 slice.156
  15.7 0.6 fusion.45
  16.4 0.7 compare_select_fusion
  17.1 0.1 fusion.40
  17.2 5.2 fusion.23
  22.4 5.4 iota_compare_fusion.17
  27.9 13.5 %fusion.28 = f32[6144,1024]{0,1:T(8,128)} fusion(s32[6144]{0:T(1024)S(1)} %copy-done.6, f32[8,1024]{1,0:T(8,128)S(1)} %copy-done.7), kind=kOutput, calls=%fused_computation.67 | convolution fusion | flops 604028928 | bytes 25223168 | tf_op jit(solution)/shard_map/dot_general | solution.py:49
  41.4 115.1 %all-gather.2.cloned.1.call-done = bf16[2,625,6144]{2,0,1:T(2,128)(2,1)} async-done(((bf16[2,625,1536]{2,0,1:T(2,128)(2,1)}), bf16[2,625,6144]{2,0,1:T(2,128)(2,1)}) %all-gather.2.cloned.1.call-update) | async-done | bytes 15360016 | tf_op jit(solution)/shard_map/all_gather | solution.py:102
  156.5 12.3 %copy.35 = bf16[2,625,6144]{2,1,0:T(8,128)(2,1)} copy(bf16[2,625,6144]{2,0,1:T(2,128)(2,1)} %all-gather.2.cloned.1.call-done) | data formatting | bytes 30720000 | tf_op jit(solution)/shard_map/all_gather | solution.py:102
  168.8 14.2 %reshape.61 = bf16[1250,6144]{1,0:T(8,128)(2,1)} reshape(bf16[2,625,6144]{2,1,0:T(8,128)(2,1)} %copy.35) | data formatting | bytes 30720000 | tf_op jit(solution)/shard_map/reshape | solution.py:40
  183.1 20.2 %convolution_convert_fusion = bf16[1024,6144]{1,0:T(8,128)(2,1)S(1)} fusion(bf16[1250,6144]{1,0:T(8,128)(2,1)} %reshape.61, bf16[625,512]{1,0:T(8,128)(2,1)S(1)} %bitcast.89, bf16[625,512]{1,0:T(8,128)(2,1)S(1)} %get-tuple-element.8, bf16[625,512]{1,0:T(8,128)(2,1)S(1)} %get-tuple-element.9), kind=kOutput, calls=%fused_computation.31 | convolution fusion | flops 15745171456 | bytes 29862912 | tf_op jit(solution)/shard_map/dot_general | solution.py:41
  203.3 4.5 copy-done.1
  207.8 0.1 fusion.42
  207.9 1.2 collective-permute-start
  209.1 1.2 collective-permute-start.1
  210.3 1.3 fusion.37
  212.2 0.0 collective-permute-done
  212.2 0.1 collective-permute-done.1
  212.3 34.0 %fusion.3 = f32[6144,2,512,1]{0,2,1,3:T(8,128)} fusion(bf16[6144,2,512]{0,2,1:T(8,128)(2,1)} %bitcast.83, bf16[6144,2,2]{0,2,1:T(2,128)(2,1)S(1)} %collective-permute-done.1, bf16[6144,2,2]{0,2,1:T(2,128)(2,1)S(1)} %collective-permute-done, f32[512]{0:T(512)S(1)} %bitcast.99, f32[512]{0:T(512)S(1)} %bitcast.100, f32[512]{0:T(512)S(1)} %bitcast.101, ...), kind=kLoop, calls=%fused_computation.13 | loop fusion | flops 125829120 | bytes 37855232 | tf_op jit(solution)/shard_map/stack | solution.py:62
  246.3 24.5 %fusion.7 = f32[6144,2,512,1]{0,2,1,3:T(8,128)} fusion(bf16[6144,2,512]{0,2,1:T(8,128)(2,1)S(1)} %bitcast.84, bf16[6144,2,2]{0,2,1:T(2,128)(2,1)S(1)} %collective-permute-done.1, bf16[6144,2,2]{0,2,1:T(2,128)(2,1)S(1)} %collective-permute-done, f32[512]{0:T(512)S(1)} %bitcast.103, f32[512]{0:T(512)S(1)} %bitcast.104, f32[512]{0:T(512)S(1)} %bitcast.105, ...), kind=kLoop, calls=%fused_computation.17 | loop fusion | flops 125829120 | bytes 37855232 | tf_op jit(solution)/shard_map/stack | solution.py:62
  270.9 34.7 %pad_maximum_fusion = f32[6144,2,512,2]{0,2,1,3:T(8,128)} fusion(f32[6144,2,512,1]{0,2,1,3:T(8,128)} %fusion.7, f32[6144,2,512,1]{0,2,1,3:T(8,128)} %fusion.3), kind=kLoop, calls=%fused_computation | loop fusion | flops 12582912 | bytes 100663296 | tf_op jit(solution)/shard_map/stack | solution.py:62
  305.6 81.9 %copy.36 = f32[6144,2,512,2]{0,3,2,1:T(2,128)} copy(f32[6144,2,512,2]{0,2,1,3:T(8,128)} %pad_maximum_fusion) | data formatting | bytes 100663296 | tf_op jit(solution)/shard_map/stack | solution.py:62
  387.5 57.2 %reshape.62 = f32[6144,2,1024]{0,2,1:T(8,128)} reshape(f32[6144,2,512,2]{0,3,2,1:T(2,128)} %copy.36) | data formatting | bytes 100663296 | tf_op jit(solution)/shard_map/reshape | solution.py:62
  444.7 40.7 %subtract_bitcast_fusion = (f32[6144,1,1024]{0,2,1:T(8,128)}, f32[6144,1,1024]{0,2,1:T(8,128)}) fusion(f32[6144,1024]{0,1:T(8,128)} %fusion.28, f32[6144,2,1024]{0,2,1:T(8,128)} %reshape.62, f32[8,1024]{1,0:T(8,128)S(1)} %copy-done.7, s32[6144]{0:T(1024)S(1)} %copy-done.6), kind=kOutput, calls=%fused_computation.21 | convolution fusion | flops 641777664 | bytes 125886464 | tf_op jit(solution)/shard_map/dot_general | solution.py:49
  485.4 34.7 %pad_maximum_fusion.1 = f32[6144,2,1024]{0,2,1:T(8,128)} fusion(f32[6144,1,1024]{0,2,1:T(8,128)} %get-tuple-element.11, f32[6144,1,1024]{0,2,1:T(8,128)} %get-tuple-element.10), kind=kLoop, calls=%fused_computation.1 | loop fusion | flops 12582912 | bytes 100663296 | tf_op jit(solution)/shard_map/stack | solution.py:67
  520.1 65.0 %fusion.8 = f32[770,2048]{1,0:T(8,128)S(1)} fusion(f32[6144,2048]{0,1:T(8,128)} %bitcast.85, pred[770,6144]{1,0:T(8,128)(4,1)} %iota_compare_fusion.17), kind=kOutput, calls=%fused_computation.23 | convolution fusion | flops 116266106880 | bytes 61370368 | tf_op jit(solution)/shard_map/dot_general | solution.py:77
  585.2 2.6 copy-done.3
  587.9 3.7 collective-permute-start.2
  591.6 0.6 slice.166
  592.3 6.3 slice.190
  598.6 6.6 copy.43
  605.2 0.0 collective-permute-done.2
  605.2 3.4 multiply_add_fusion
  608.6 2.2 collective-permute-start.3
  610.7 0.4 collective-permute-start.4
  611.2 0.9 collective-permute-done.3
  612.1 1.4 collective-permute-done.4
  613.5 5.6 add_bitcast_fusion.2
  619.1 6.8 add_bitcast_fusion.1
  625.9 8.8 %pad_maximum_fusion.4 = f32[768,2,1024,2]{0,2,1,3:T(8,128)} fusion(f32[768,2,1024,1]{0,2,1,3:T(8,128)} %add_bitcast_fusion.1, f32[768,2,1024,1]{0,2,1,3:T(8,128)S(1)} %add_bitcast_fusion.2), kind=kLoop, calls=%fused_computation.29 | loop fusion | flops 3145728 | bytes 25165824 | tf_op jit(solution)/shard_map/stack | solution.py:62
  634.7 21.0 %copy.38 = f32[768,2,1024,2]{0,1,3,2:T(2,128)S(1)} copy(f32[768,2,1024,2]{0,2,1,3:T(8,128)} %pad_maximum_fusion.4) | data formatting | bytes 25165824 | tf_op jit(solution)/shard_map/stack | solution.py:62
  655.8 11.0 %fusion.41 = (f32[768,1,2048]{0,1,2:T(1,128)}, f32[768,1,2048]{0,1,2:T(1,128)}) fusion(f32[768,2,2048]{0,1,2:T(2,128)S(1)} %bitcast.86), kind=kLoop, calls=%fused_computation.88 | loop fusion | bytes 25165824 | tf_op jit(solution)/shard_map/slice | solution.py:65
  666.8 15.8 %copy.46 = f32[768,1,2048]{2,0,1:T(8,128)} copy(f32[768,1,2048]{0,1,2:T(1,128)} %get-tuple-element.14) | data formatting | bytes 12582912
  682.6 15.7 %copy.47 = f32[768,1,2048]{2,0,1:T(8,128)} copy(f32[768,1,2048]{0,1,2:T(1,128)} %get-tuple-element.15) | data formatting | bytes 12582912
  698.3 10.2 %fusion.13 = (f32[768,1,2048]{2,0,1:T(8,128)S(1)}, f32[768,1,2048]{2,0,1:T(8,128)}) fusion(f32[768,2048]{1,0:T(8,128)} %fusion.23, f32[768,1,2048]{2,0,1:T(8,128)} %copy.47, f32[768,1,2048]{2,0,1:T(8,128)} %copy.46, f32[8,2048]{1,0:T(8,128)S(1)} %copy-done.5, s32[768]{0:T(1024)S(1)} %copy-done.14), kind=kOutput, calls=%fused_computation.41 | convolution fusion | flops 160438272 | bytes 31525888 | tf_op jit(solution)/shard_map/dot_general | solution.py:49
  708.5 8.9 %pad_maximum_fusion.5 = f32[768,2,2048]{2,0,1:T(8,128)} fusion(f32[768,1,2048]{2,0,1:T(8,128)} %get-tuple-element.13, f32[768,1,2048]{2,0,1:T(8,128)S(1)} %get-tuple-element.12), kind=kLoop, calls=%fused_computation.30 | loop fusion | flops 3145728 | bytes 25165824 | tf_op jit(solution)/shard_map/stack | solution.py:67
  717.4 12.7 %copy.41 = f32[768,2,2048]{0,2,1:T(8,128)} copy(f32[768,2,2048]{2,0,1:T(8,128)} %pad_maximum_fusion.5) | data formatting | bytes 25165824 | tf_op jit(solution)/shard_map/stack | solution.py:67
  730.1 9.8 %fusion.25 = f32[98,4096]{1,0:T(8,128)S(1)} fusion(f32[768,4096]{0,1:T(8,128)} %bitcast.87, s32[768]{0:T(1024)S(1)} %copy-done.15), kind=kOutput, calls=%fused_computation.63 | convolution fusion | flops 3699451392 | bytes 14191616 | tf_op jit(solution)/shard_map/dot_general | solution.py:77
  740.0 3.3 collective-permute-start.5
  743.4 0.6 compare_convert_fusion
  744.0 10.3 %copy.42 = f32[768,2,1024]{2,1,0:T(2,128)} copy(f32[768,2,1024]{0,2,1:T(8,128)} %copy-done) | data formatting | bytes 12582912
  754.3 0.1 slice.206
  754.4 1.3 slice.174
  755.7 0.0 collective-permute-done.5
  755.8 1.8 multiply_add_fusion.1
  (38 shorter events, 0.2 us)
Async XLA Ops:
  7.2 10.0 %copy-start.13 = (s32[768]{0:T(1024)S(1)}, s32[768]{0:T(1024)}, u32[]{:S(2)}) copy-start(s32[768]{0:T(1024)} %param.15) | copy-start | bytes 9220
  7.2 10.0 %copy-start.4 = (f32[8,2048]{1,0:T(8,128)S(1)}, f32[8,2048]{1,0:T(8,128)}, u32[]{:S(2)}) copy-start(f32[8,2048]{1,0:T(8,128)} %param.19) | copy-start | bytes 196612
  7.2 20.7 %copy-start.6 = (s32[6144]{0:T(1024)S(1)}, s32[6144]{0:T(1024)}, u32[]{:S(2)}) copy-start(s32[6144]{0:T(1024)} %param.13) | copy-start | bytes 73732
  7.2 20.7 %copy-start.7 = (f32[8,1024]{1,0:T(8,128)S(1)}, f32[8,1024]{1,0:T(8,128)}, u32[]{:S(2)}) copy-start(f32[8,1024]{1,0:T(8,128)} %param.17) | copy-start | bytes 98308
  7.2 149.3 %all-gather.2.cloned.1.call-start = ((), (), s32[]{:S(2)}) async-start(), calls=%async_computation | async-start | bytes 19200000 | tf_op jit(solution)/shard_map/all_gather | solution.py:102
  183.1 27.2 %copy-start.16 = (s32[768]{0:T(1024)S(1)}, s32[768]{0:T(1024)}, u32[]{:S(2)}) copy-start(s32[768]{0:T(1024)} %param.14) | copy-start | bytes 9220
  203.3 4.5 copy-start.1
  207.9 4.3 collective-permute-start
  209.1 3.2 collective-permute-start.1
  212.3 34.0 %copy-start.2 = (bf16[1024,6144]{1,0:T(8,128)(2,1)S(1)}, bf16[1024,6144]{1,0:T(8,128)(2,1)}, u32[]{:S(2)}) copy-start(bf16[1024,6144]{1,0:T(8,128)(2,1)} %copy-done.1) | copy-start | bytes 37748740
  520.1 71.5 %copy-start.8 = (f32[4,2048]{1,0:T(4,128)S(1)}, f32[4,2048]{1,0:T(4,128)}, u32[]{:S(2)}) copy-start(f32[4,2048]{1,0:T(4,128)} %param.18) | copy-start | bytes 98308
  585.2 2.7 copy-start.3
  587.9 17.3 %collective-permute-start.2 = (f32[2,1024]{1,0:T(2,128)S(1)}, f32[2,1024]{1,0:T(2,128)S(1)}, u32[]{:S(2)}, u32[]{:S(2)}) collective-permute-start(f32[2,1024]{1,0:T(2,128)S(1)} %squeeze.28), channel_id=1, source_target_pairs={{4,0},{8,4},{12,8},{16,12},{20,16},{24,20},{28,24},{5,1},{9,5},{13... | collective-permute-start | bytes 24584 | tf_op jit(solution)/shard_map/ppermute | solution.py:26
  598.6 14.9 %copy-start.9 = (f32[1,1024]{1,0:T(1,128)S(1)}, f32[1,1024]{1,0:T(1,128)}, u32[]{:S(2)}) copy-start(f32[1,1024]{1,0:T(1,128)} %get-tuple-element.22) | copy-start | bytes 12292
  598.6 14.9 %copy-start.10 = (f32[1,1024]{1,0:T(1,128)S(1)}, f32[1,1024]{1,0:T(1,128)}, u32[]{:S(2)}) copy-start(f32[1,1024]{1,0:T(1,128)} %get-tuple-element.23) | copy-start | bytes 12292
  598.6 14.9 %copy-start.11 = (f32[1,1024]{1,0:T(1,128)S(1)}, f32[1,1024]{1,0:T(1,128)}, u32[]{:S(2)}) copy-start(f32[1,1024]{1,0:T(1,128)} %get-tuple-element.24) | copy-start | bytes 12292
  598.6 14.9 %copy-start.12 = (f32[1,1024]{1,0:T(1,128)S(1)}, f32[1,1024]{1,0:T(1,128)}, u32[]{:S(2)}) copy-start(f32[1,1024]{1,0:T(1,128)} %get-tuple-element.25) | copy-start | bytes 12292
  608.5 10.5 %copy-start = (f32[768,2,1024]{0,2,1:T(8,128)}, f32[768,2,1024]{0,2,1:T(8,128)S(1)}, u32[]{:S(2)}) copy-start(f32[768,2,1024]{0,2,1:T(8,128)S(1)} %multiply_add_fusion) | copy-start | bytes 18874372
  608.6 3.5 collective-permute-start.3
  610.7 2.7 collective-permute-start.4
  666.8 31.5 %copy-start.5 = (f32[8,2048]{1,0:T(8,128)S(1)}, f32[8,2048]{1,0:T(8,128)}, u32[]{:S(2)}) copy-start(f32[8,2048]{1,0:T(8,128)} %param.19) | copy-start | bytes 196612
  666.8 31.5 %copy-start.14 = (s32[768]{0:T(1024)S(1)}, s32[768]{0:T(1024)}, u32[]{:S(2)}) copy-start(s32[768]{0:T(1024)} %param.15) | copy-start | bytes 9220
  717.4 12.7 %copy-start.15 = (s32[768]{0:T(1024)S(1)}, s32[768]{0:T(1024)}, u32[]{:S(2)}) copy-start(s32[768]{0:T(1024)} %get-tuple-element.38) | copy-start | bytes 9220
  740.0 15.7 %collective-permute-start.5 = (f32[2,2048]{1,0:T(2,128)S(1)}, f32[2,2048]{1,0:T(2,128)S(1)}, u32[]{:S(2)}, u32[]{:S(2)}) collective-permute-start(f32[2,2048]{1,0:T(2,128)S(1)} %squeeze.31), channel_id=1, source_target_pairs={{4,0},{8,4},{12,8},{16,12},{20,16},{24,20},{28,24},{5,1},{9,5},{13... | collective-permute-start | bytes 49160 | tf_op jit(solution)/shard_map/ppermute | solution.py:26
Sparse Core Ops, SparseCore 0:
  9.9 146.6 all-gather.1
where the time goes:
time: 772 us; the launch traced here: 765 us
  local copies, waits for them, and re-layouts  283 us (37%)
  other arithmetic  171 us (22%)
  matrix products  165 us (21%)
  waiting for transfers between devices  118 us (15%)
  between operations  15.2 us (2%)
  starting transfers between devices  12.1 us (2%)
    all_gather x1, waiting for transfers between devices, body(): lax.all_gather(coefficients, 'angle', axis=2, tiled=True)  115 us
    another operation x6, other arithmetic, upsample_shift(): jnp.stack([even_sum, odd_sum], axis=-1)  114 us
    another operation x2, local copies, waits for them, and re-layouts, upsample_shift(): jnp.stack([even_sum, odd_sum], axis=-1)  103 us
    dot_general x2, matrix products, slot_sums(): summed = jnp.dot(selector, flat, precision=lax.Precision.HIGHEST)  74.9 us
    dot_general x4, matrix products, octant_rows(): return jnp.dot(selector, table, precision=lax.Precision.HIGHEST)  69.7 us
    reshape x1, local copies, waits for them, and re-layouts, upsample_shift(): jnp.stack([even_sum, odd_sum], axis=-1)  57.2 us
    unnamed x38, local copies, waits for them, and re-layouts  49.2 us
    another operation x2, other arithmetic, upsample_shift(): jnp.stack([real_part * cos_rows - imag_part * sin_rows, real_part * sin_r...  43.6 us
  transfers between devices with their start and end apart: 7, of which 4 were waited for; matrix products, arithmetic and copies ran while one was open for 8% of the time, Pallas kernels for 0%

commit v1 on v0

v1 whole, which is shorter than its diff:
```python
import functools

import jax
import jax.numpy as jnp
from jax import lax
from jax.experimental import pallas as pl
from jax.experimental.pallas import tpu as pltpu
from jax.sharding import PartitionSpec as P

BF = jnp.bfloat16
F32 = jnp.float32
PAD = 128
CHUNK = 256


def passed_along(array, axis, by):
    peers = lax.axis_size(axis)
    pairs = [(i, i + by) for i in range(peers) if 0 <= i + by < peers]
    return lax.ppermute(array, axis, pairs)


def widened(cells, left, right, axis):
    count = lax.axis_size(axis)
    width = cells.shape[-1]
    head = cells[..., :right]
    tail = cells[..., width - left :]
    before = lax.ppermute(tail, axis, [(i, (i + 1) % count) for i in range(count)])
    after = lax.ppermute(head, axis, [((i + 1) % count, i) for i in range(count)])
    fill = jnp.zeros(cells.shape[:-1] + (PAD - left - right,), cells.dtype)
    return jnp.concatenate([before, cells, after, fill], axis=-1)


def split(array):
    high = array.astype(BF)
    return high, (array - high.astype(F32)).astype(BF)


def split_table(array):
    high = lax.reduce_precision(array, 8, 7)
    return high.astype(BF), (array - high).astype(BF)


def band(weights, shift):
    columns = weights.shape[1]
    rows = jnp.arange(CHUNK, dtype=jnp.int32)[:, None]
    first = (jnp.arange(columns, dtype=jnp.int32)[None, :] % CHUNK) // 2 + shift
    total = jnp.zeros((CHUNK, columns), F32)
    for tap in range(4):
        total = total + jnp.where(rows == first + tap, weights[tap][None, :], 0.0)
    return jnp.stack(split_table(total))


def phase_table(phase):
    both = jnp.concatenate([jnp.cos(phase), jnp.sin(phase)], axis=1)
    return jnp.concatenate(split_table(both), axis=0)


def dot(a, b):
    return jnp.dot(a, b, preferred_element_type=F32)


def dot_lead(a, b):
    return lax.dot_general(a, b, (((0,), (0,)), ((), ())), preferred_element_type=F32)


def octant_hot(octant):
    rows = lax.broadcasted_iota(jnp.int32, (16, octant.shape[1]), 0)
    return ((rows % 8) == octant).astype(F32).astype(BF)


def level_one_kernel(window, meta, coef, weights, bands, table, target, octant, sums, carry):
    tile = pl.program_id(0)
    wide = sums.shape[2]
    ext = weights.shape[2] // 2
    keep = window - 8

    @pl.when(tile == 0)
    def _():
        sums[...] = jnp.zeros_like(sums)

    @pl.when(tile < meta[0])
    def _():
        base = pl.multiple_of(meta[1 + tile], 8)
        leaf = dot_lead(coef[0, 0], weights[0]) + dot_lead(coef[0, 1], weights[1])
        leaf = leaf.astype(BF)
        count = leaf.shape[0]
        hot = octant_hot(octant[0])
        rows = lax.broadcasted_iota(jnp.int32, (window, count), 0)
        select = (rows == target[0] - base).astype(F32).astype(BF)
        for lo in range(0, wide, CHUNK):
            hi = min(lo + CHUNK, wide)
            start = lo // 2
            stop = min(start + CHUNK, ext)
            deep = stop - start
            wh = bands[0, :deep, lo:hi]
            wl = bands[1, :deep, lo:hi]
            xr = leaf[:, start:stop]
            xi = leaf[:, ext + start : ext + stop]
            ur = dot(xr, wh) + dot(xr, wl)
            ui = dot(xi, wh) + dot(xi, wl)
            cosine = dot_lead(hot, table[:, lo:hi])
            sine = dot_lead(hot, table[:, wide + lo : wide + hi])
            for part, value in ((0, ur * cosine - ui * sine), (1, ur * sine + ui * cosine)):
                res = dot(select, value.astype(BF))
                sums[part, pl.ds(base, keep), lo:hi] += res[:keep]

                @pl.when(tile == 0)
                def _():
                    carry[part, :, lo:hi] = res[keep:]


def level_one(gathered, weights, bands, table, leaf_parent, leaf_octant, slots_one):
    groups, _, order, per = gathered.shape
    leaves = groups * per
    tile = next(t for t in (256, 128) if per % t == 0)
    window = tile // 4 + 24
    tiles = leaves // tile
    each = per // tile
    wide = bands.shape[2]
    live = jnp.sum((leaf_parent != slots_one).astype(jnp.int32))
    live_tiles = (live + tile - 1) // tile
    first = leaf_parent.reshape(tiles, tile)[:, 0]
    base = jnp.clip(first, 0, slots_one - 1) // 8 * 8
    meta = jnp.concatenate([live_tiles[None], base]).astype(jnp.int32)
    target = jnp.where(
        leaf_parent == slots_one, -8, jnp.where(leaf_parent < 0, window - 1, leaf_parent)
    )

    def at(i, meta):
        return jnp.minimum(i, jnp.maximum(meta[0] - 1, 0))

    return pl.pallas_call(
        functools.partial(level_one_kernel, window),
        grid_spec=pltpu.PrefetchScalarGridSpec(
            num_scalar_prefetch=1,
            grid=(tiles,),
            in_specs=[
                pl.BlockSpec(
                    (1, 2, order, tile), lambda i, m: (at(i, m) // each, 0, 0, at(i, m) % each)
                ),
                pl.BlockSpec(weights.shape, lambda i, m: (0, 0, 0)),
                pl.BlockSpec(bands.shape, lambda i, m: (0, 0, 0)),
                pl.BlockSpec(table.shape, lambda i, m: (0, 0)),
                pl.BlockSpec((1, 1, tile), lambda i, m: (at(i, m), 0, 0)),
                pl.BlockSpec((1, 1, tile), lambda i, m: (at(i, m), 0, 0)),
            ],
            out_specs=[
                pl.BlockSpec((2, slots_one + window, wide), lambda i, m: (0, 0, 0)),
                pl.BlockSpec((2, 8, wide), lambda i, m: (0, 0, 0)),
            ],
        ),
        out_shape=[
            jax.ShapeDtypeStruct((2, slots_one + window, wide), F32),
            jax.ShapeDtypeStruct((2, 8, wide), F32),
        ],
        compiler_params=pltpu.CompilerParams(vmem_limit_bytes=56 * 2**20),
        cost_estimate=pl.CostEstimate(
            flops=2 * leaves * order * 8 * weights.shape[2],
            bytes_accessed=2 * gathered.size,
            transcendentals=0,
        ),
    )(
        meta,
        gathered,
        weights,
        bands,
        table,
        target.reshape(tiles, 1, tile),
        leaf_octant.reshape(tiles, 1, tile),
    )


def level_two_kernel(meta, sums, incoming, bands, table, target, octant, one, two):
    tile = pl.program_id(0)
    count = sums.shape[1]
    wide = bands.shape[2]
    near = one.shape[2]
    slots = lax.broadcasted_iota(jnp.int32, (count, 1), 0) + tile * count
    last = slots == meta[1]
    fields = []
    for part in range(2):
        field = sums[part] + jnp.where(last, incoming[part : part + 1], 0.0)
        fields.append(field)
        one[:, part, :] = field[:, 2 : 2 + near]

    @pl.when(tile == 0)
    def _():
        two[...] = jnp.zeros_like(two)

    @pl.when(tile < meta[0])
    def _():
        rows = two.shape[1]
        hot = octant_hot(octant[0])
        select = lax.broadcasted_iota(jnp.int32, (rows, count), 0) == target[0]
        select = select.astype(F32).astype(BF)
        halves = [split(field) for field in fields]
        for lo in range(0, wide, CHUNK):
            hi = min(lo + CHUNK, wide)
            start = lo // 2
            stop = start + CHUNK
            wh = bands[0, :, lo:hi]
            wl = bands[1, :, lo:hi]
            ups = []
            for xh, xl in halves:
                xh = xh[:, start:stop]
                ups.append(dot(xh, wh) + dot(xh, wl) + dot(xl[:, start:stop], wh))
            ur, ui = ups
            cosine = dot_lead(hot, table[:, lo:hi])
            sine = dot_lead(hot, table[:, wide + lo : wide + hi])
            for part, value in ((0, ur * cosine - ui * sine), (1, ur * sine + ui * cosine)):
                vh, vl = split(value)
                two[part, :, lo:hi] += dot(select, vh) + dot(select, vl)


def level_two(sums, incoming, live, bands, table, box_parent, box_octant, slots_two):
    slots_one = box_parent.shape[0]
    ext = sums.shape[2]
    tile = next(t for t in (128, 64, 32, 8) if slots_one % t == 0)
    tiles = slots_one // tile
    rows = (slots_two + 7) // 8 * 8 + 8
    wide = bands.shape[2]
    meta = jnp.stack([(live + tile - 1) // tile, live - 1]).astype(jnp.int32)
    target = jnp.where(
        box_parent == slots_two, -8, jnp.where(box_parent < 0, rows - 1, box_parent)
    )
    return pl.pallas_call(
        level_two_kernel,
        grid_spec=pltpu.PrefetchScalarGridSpec(
            num_scalar_prefetch=1,
            grid=(tiles,),
            in_specs=[
                pl.BlockSpec((2, tile, ext), lambda i, m: (0, i, 0)),
                pl.BlockSpec((2, ext), lambda i, m: (0, 0)),
                pl.BlockSpec(bands.shape, lambda i, m: (0, 0, 0)),
                pl.BlockSpec(table.shape, lambda i, m: (0, 0)),
                pl.BlockSpec((1, 1, tile), lambda i, m: (i, 0, 0)),
                pl.BlockSpec((1, 1, tile), lambda i, m: (i, 0, 0)),
            ],
            out_specs=[
                pl.BlockSpec((tile, 2, ext - PAD), lambda i, m: (i, 0, 0)),
                pl.BlockSpec((2, rows, wide), lambda i, m: (0, 0, 0)),
            ],
        ),
        out_shape=[
            jax.ShapeDtypeStruct((slots_one, 2, ext - PAD), F32),
            jax.ShapeDtypeStruct((2, rows, wide), F32),
        ],
        compiler_params=pltpu.CompilerParams(vmem_limit_bytes=56 * 2**20),
    )(
        meta,
        sums,
        incoming,
        bands,
        table,
        target.reshape(tiles, 1, tile),
        box_octant.reshape(tiles, 1, tile),
    )


def body(
    coefficients,
    plane_map,
    leaf_parent,
    leaf_octant,
    box_parent,
    box_octant,
    interp_one,
    phase_one,
    interp_two,
    phase_two,
):
    slots_one = box_parent.shape[0]
    slots_two = slots_one // 8
    gathered = lax.all_gather(coefficients, "angle", axis=0)
    plane = widened(plane_map, 2, 3, "angle")
    weights = jnp.stack(
        [
            jnp.concatenate([plane[0], plane[1]], axis=1),
            jnp.concatenate([-plane[1], plane[0]], axis=1),
        ]
    )
    near = widened(jnp.concatenate([interp_one, phase_one], axis=0), 2, 2, "angle")
    sums, carry = level_one(
        gathered,
        weights,
        band(near[:4], 0),
        phase_table(near[4:]),
        leaf_parent,
        leaf_octant,
        slots_one,
    )
    incoming = passed_along(carry[:, 7], "box", -1)
    live = jnp.sum((box_parent != slots_two).astype(jnp.int32))
    signature_one, sums_two = level_two(
        sums,
        incoming,
        live,
        band(interp_two, 1),
        phase_table(phase_two),
        box_parent,
        box_octant,
        slots_two,
    )
    incoming_two = passed_along(sums_two[:, -1], "box", -1)
    last_two = jnp.max(jnp.where(box_parent < slots_two, box_parent, -1))
    hit = jnp.arange(slots_two, dtype=jnp.int32)[:, None, None] == last_two
    signature_two = jnp.swapaxes(sums_two[:, :slots_two], 0, 1) + jnp.where(
        hit, incoming_two[None], 0.0
    )
    return (signature_one, signature_two)


def solution(mesh):
    in_specs = (
        P(None, None, ("box", "angle")),
        P(None, None, "angle"),
        P("box"),
        P("box"),
        P("box"),
        P("box"),
        P(None, "angle"),
        P(None, "angle"),
        P(None, "angle"),
        P(None, "angle"),
    )
    out_specs = (P("box", None, "angle"), P("box", None, "angle"))
    return jax.shard_map(body, mesh=mesh, in_specs=in_specs, out_specs=out_specs, check_vma=False)
```

time: 772 us -> 276 us (0.36)
  local copies, waits for them, and re-layouts: 283 us -> 12.5 us
  matrix products: 165 us -> 0 us
  other arithmetic: 171 us -> 15 us
  Pallas kernels: 0 us -> 71.1 us
  waiting for transfers between devices: 118 us -> 134 us
  starting transfers between devices: 12.1 us -> 24.4 us
    dot_general x7 -> x0, matrix products: 165 us -> none  [the longest x2 74.9 us: slot_sums(): summed = jnp.dot(selector, flat, precision=lax.Precision.HIGHEST)]
    another operation x8 -> x5, other arithmetic: 158 us -> 5.56 us  [the longest x2 2.63 us: band(): return jnp.stack(split_table(total))]
    another operation x3 -> x0, local copies, waits for them, and re-layouts: 116 us -> none  [the longest x2 103 us: upsample_shift(): jnp.stack([even_sum, odd_sum], axis=-1)]
    pallas_call x0 -> x2, Pallas kernels: none -> 71.1 us  [the longest x1 49.3 us: level_one(): pl.pallas_call(functools.partial(level_one_kernel, window), grid_spec=plt...]
    reshape x2 -> x3, local copies, waits for them, and re-layouts: 71.4 us -> 1.21 us  [the longest x1 0.6 us: level_two(): box_octant.reshape(tiles, 1, tile)]
    unnamed x38 -> x22, local copies, waits for them, and re-layouts: 49.2 us -> 8.52 us
    slice x18 -> x5, local copies, waits for them, and re-layouts: 34.4 us -> 1.2 us  [the longest x1 0.92 us: body(): incoming_two = passed_along(sums_two[:, -1], 'box', -1)]
    ppermute x2, starting transfers between devices: 7.08 us -> 19.5 us  [passed_along(): return lax.ppermute(array, axis, pairs)]
  transfers between devices with their start and end apart: 7 -> 7, of which waited for: 4 -> 4; matrix products, arithmetic and copies ran while one was open for 8% -> 6% of each run, Pallas kernels for 0% -> 0%
where the time goes in v1:
time: 276 us; the launch traced here: 274 us
  waiting for transfers between devices  134 us (49%)
  Pallas kernels  71.1 us (26%)
  starting transfers between devices  24.4 us (9%)
  between operations  16.3 us (6%)
  other arithmetic  15 us (5%)
  local copies, waits for them, and re-layouts  12.5 us (5%)
    all_gather x1, waiting for transfers between devices, body(): gathered = lax.all_gather(coefficients, 'angle', axis=0)  126 us
    pallas_call x1, Pallas kernels, level_one(): pl.pallas_call(functools.partial(level_one_kernel, window), grid_spec=plt...  49.3 us
    pallas_call x1, Pallas kernels, level_two(): pl.pallas_call(level_two_kernel, grid_spec=pltpu.PrefetchScalarGridSpec(n...  21.8 us
    ppermute x2, starting transfers between devices, passed_along(): return lax.ppermute(array, axis, pairs)  19.5 us
    unnamed x22, local copies, waits for them, and re-layouts  8.52 us
    ppermute x2, waiting for transfers between devices, widened(): lax.ppermute(head, axis, [((i + 1) % count, i) for i in range(count)])  5.82 us
  transfers between devices with their start and end apart: 7, of which 4 were waited for; matrix products, arithmetic and copies ran while one was open for 6% of the time, Pallas kernels for 0%

profile of v1, /device:TPU:9, one launch (start us, length us, event | category | flops | bytes accessed | tf_op | source)
XLA Modules:
  0.0 273.7 jit_solution(6152386797817389801)
XLA Ops:
  7.2 0.0 all-gather.3.cloned.1.call-start
  7.2 4.6 %copy.30 = bf16[2,625,1536]{2,1,0:T(8,128)(2,1)} copy(bf16[2,625,1536]{2,0,1:T(2,128)(2,1)} %param.10) | data formatting | bytes 7680000 | tf_op args[0]
  11.8 0.0 copy-start.4
  11.8 0.0 copy-start
  11.8 0.0 all-gather.3.cloned.1.call-update
  11.8 0.7 copy-done.1
  12.6 0.0 copy-done.4
  12.6 0.1 fusion.9
  12.6 1.2 collective-permute-start.2
  13.8 0.0 copy-start.2
  13.8 0.0 copy-start.8
  13.8 0.0 copy-start.5
  13.8 1.2 collective-permute-start.3
  15.0 0.0 copy-done
  15.0 0.2 copy.31
  15.2 0.2 slice.84
  15.4 0.4 collective-permute-start
  15.8 2.1 collective-permute-start.1
  17.9 0.0 copy-done.2
  17.9 1.2 fusion.4
  19.8 0.0 copy-done.8
  19.8 0.7 fusion.21
  21.8 0.1 pad.23.clone
  21.9 0.1 fusion.5
  22.1 0.6 pad_add_fusion.1.meta
  22.7 0.0 copy-done.5
  22.8 1.2 reduce-precision_convert_fusion
  24.0 0.0 copy-start.3
  24.0 1.5 pad_maximum_fusion.1.bands
  25.5 0.0 copy-done.3
  25.5 0.2 fusion.24
  25.8 0.7 pad_maximum_fusion.4.table
  26.5 0.0 collective-permute-done.2
  26.5 0.0 collective-permute-done.3
  26.5 0.1 concatenate.35
  26.6 0.1 slice_reduce_fusion.3
  26.6 0.1 slice_cosine_fusion
  26.8 0.6 pad_maximum_fusion.7.table
  27.4 0.7 reduce-precision_convert_fusion.1
  28.2 1.1 pad_maximum_fusion.2.bands
  29.3 0.0 collective-permute-done
  29.3 5.8 %collective-permute-done.1 = bf16[2,625,3]{2,1,0:T(8,128)(2,1)S(1)} collective-permute-done((bf16[2,625,3]{2,1,0:T(8,128)(2,1)S(1)}, bf16[2,625,3]{2,1,0:T(8,128)(2,1)S(1)}, u32[]{:S(2)}, u32[]{:S(2)}) %collective-permute-start.1) | collective-permute-done | bytes 7532 | tf_op jit(solution)/shard_map/ppermute | solution.py:28
  35.1 1.1 maximum_maximum_fusion
  36.2 0.1 fusion.23
  36.3 0.1 slice_bitcast_fusion
  36.4 0.3 maximum_bitcast_fusion
  36.8 2.0 pad_maximum_fusion.weights
  38.8 126.2 %all-gather.3.cloned.1.call-done = bf16[8,625,1536]{2,1,0:T(8,128)(2,1)} async-done(((bf16[2,625,1536]{2,1,0:T(8,128)(2,1)}), bf16[8,625,1536]{2,1,0:T(8,128)(2,1)}) %all-gather.3.cloned.1.call-update) | async-done | bytes 15360016 | tf_op jit(solution)/shard_map/all_gather | solution.py:274
  165.0 49.3 %shard_map.113 = (f32[2,856,1152]{2,1,0:T(8,128)}, f32[2,8,1152]{2,1,0:T(8,128)}) custom-call(s32[25]{0:T(128)} %pad_add_fusion.1.meta, bf16[4,2,625,1536]{3,2,1,0:T(8,128)(2,1)} %bitcast.33, bf16[2,625,1280]{2,1,0:T(8,128)(2,1)} %pad_maximum_fusion.weights, bf16[2,256,1152]{2,1,0:T(8,128)(2,1)} %pad_maximum_fusion.2.bands, ...), custom_call_target="tpu_custom_call" | custom-call | flops 78643200000 | bytes 15360000 | tf_op jit(solution)/shard_map/pallas_call | solution.py:132
  214.3 0.9 copy.34
  215.2 16.1 %collective-permute-start.4 = (f32[2,1152]{1,0:T(2,128)S(1)}, f32[2,1152]{1,0:T(2,128)S(1)}, u32[]{:S(2)}, u32[]{:S(2)}) collective-permute-start(f32[2,1152]{1,0:T(2,128)S(1)} %slice_bitcast_fusion.2), channel_id=1, source_target_pairs={{4,0},{8,4},{12,8},{16,12},{20,16},{24,20},{28,24},{5,1},{9,5},{13... | collective-permute-start | bytes 27656 | tf_op jit(solution)/shard_map/ppermute | solution.py:19
  231.3 0.6 pad_add_fusion.meta
  231.9 0.6 reshape.1029.target
  232.5 0.0 copy-done.7
  232.5 0.6 reshape.1030.octant
  233.1 0.4 collective-permute-done.4.incoming
  233.6 0.6 copy-done.6
  234.2 21.8 %shard_map.114 = (f32[768,2,1024]{2,1,0:T(2,128)}, f32[2,104,2048]{2,1,0:T(8,128)}) custom-call(s32[2]{0:T(128)} %pad_add_fusion.meta, f32[2,856,1152]{2,1,0:T(8,128)} %get-tuple-element.6.sums, f32[2,1152]{1,0:T(2,128)} %copy-done.6, bf16[2,256,2048]{2,1,0:T(8,128)(2,1)} %pad_maximum_fusion.1.bands, bf16[16,4096]{1,0:T(8,128)(2,1)} %pad_maximum_fusion.4.table, ...), custom_call_target="tpu_custom_call" | custom-call | tf_op jit(solution)/shard_map/pallas_call | solution.py:226
  256.0 0.9 slice.82
  256.9 3.4 %collective-permute-start.5 = (f32[2,2048]{1,0:T(2,128)S(1)}, f32[2,2048]{1,0:T(2,128)S(1)}, u32[]{:S(2)}, u32[]{:S(2)}) collective-permute-start(f32[2,2048]{1,0:T(2,128)S(1)} %bitcast.32), channel_id=1, source_target_pairs={{4,0},{8,4},{12,8},{16,12},{20,16},{24,20},{28,24},{5,1},{9,5},{13... | collective-permute-start | bytes 49160 | tf_op jit(solution)/shard_map/ppermute | solution.py:19
  260.4 0.6 iota_compare_fusion.8
  261.0 1.9 collective-permute-done.5
  262.9 1.6 bitcast_add_fusion
  264.5 2.4 copy.35
  (18 shorter events, 0.2 us)
Async XLA Ops:
  7.2 157.8 %all-gather.3.cloned.1.call-start = ((), (), s32[]{:S(2)}) async-start(), calls=%async_computation | async-start | bytes 19415040 | tf_op jit(solution)/shard_map/all_gather | solution.py:274
  11.8 0.8 copy-start.1
  11.8 0.8 copy-start.4
  11.8 3.2 %copy-start = (bf16[2,625,512]{2,0,1:T(2,128)(2,1)S(1)}, bf16[2,625,512]{2,0,1:T(2,128)(2,1)}, u32[]{:S(2)}) copy-start(bf16[2,625,512]{2,0,1:T(2,128)(2,1)} %param.11) | copy-start | bytes 3840004
  12.6 13.8 %collective-permute-start.2 = (f32[12,2]{1,0:T(8,128)S(1)}, f32[12,2]{1,0:T(8,128)S(1)}, u32[]{:S(2)}, u32[]{:S(2)}) collective-permute-start(f32[12,2]{1,0:T(8,128)S(1)} %get-tuple-element.41), channel_id=1, source_target_pairs={{0,1},{1,2},{2,3},{3,0},{4,5},{5,6},{6,7},{7,4},{8,9},{9,10},{10,1... | collective-permute-start | bytes 296 | tf_op jit(solution)/shard_map/ppermute | solution.py:27
  13.8 4.0 %copy-start.2 = (s32[6144]{0:T(1024)S(1)}, s32[6144]{0:T(1024)}, u32[]{:S(2)}) copy-start(s32[6144]{0:T(1024)} %param.12) | copy-start | bytes 73732
  13.8 6.0 %copy-start.8 = (s32[768]{0:T(1024)S(1)}, s32[768]{0:T(1024)}, u32[]{:S(2)}) copy-start(s32[768]{0:T(1024)} %param.14) | copy-start | bytes 9220
  13.8 8.9 %copy-start.5 = (f32[4,2048]{1,0:T(4,128)S(1)}, f32[4,2048]{1,0:T(4,128)}, u32[]{:S(2)}) copy-start(f32[4,2048]{1,0:T(4,128)} %param.18) | copy-start | bytes 98308
  13.8 12.6 %collective-permute-start.3 = (f32[12,2]{1,0:T(8,128)S(1)}, f32[12,2]{1,0:T(8,128)S(1)}, u32[]{:S(2)}, u32[]{:S(2)}) collective-permute-start(f32[12,2]{1,0:T(8,128)S(1)} %get-tuple-element.40), channel_id=1, source_target_pairs={{1,0},{2,1},{3,2},{0,3},{5,4},{6,5},{7,6},{4,7},{9,8},{10,9},{11,1... | collective-permute-start | bytes 296 | tf_op jit(solution)/shard_map/ppermute | solution.py:28
  15.4 13.9 %collective-permute-start = (bf16[2,625,2]{2,1,0:T(8,128)(2,1)S(1)}, bf16[2,625,2]{2,1,0:T(8,128)(2,1)S(1)}, u32[]{:S(2)}, u32[]{:S(2)}) collective-permute-start(bf16[2,625,2]{2,1,0:T(8,128)(2,1)S(1)} %slice.84), channel_id=1, source_target_pairs={{0,1},{1,2},{2,3},{3,0},{4,5},{5,6},{6,7},{7,4},{8,9},{9,10},{10,1... | collective-permute-start | bytes 15008 | tf_op jit(solution)/shard_map/ppermute | solution.py:27
  15.8 19.3 %collective-permute-start.1 = (bf16[2,625,3]{2,1,0:T(8,128)(2,1)S(1)}, bf16[2,625,3]{2,1,0:T(8,128)(2,1)S(1)}, u32[]{:S(2)}, u32[]{:S(2)}) collective-permute-start(bf16[2,625,3]{2,1,0:T(8,128)(2,1)S(1)} %slice.85), channel_id=1, source_target_pairs={{1,0},{2,1},{3,2},{0,3},{5,4},{6,5},{7,6},{4,7},{9,8},{10,9},{11,1... | collective-permute-start | bytes 22508 | tf_op jit(solution)/shard_map/ppermute | solution.py:28
  24.0 1.5 copy-start.3
  165.0 67.6 %copy-start.7 = (s32[768]{0:T(1024)S(1)}, s32[768]{0:T(1024)}, u32[]{:S(2)}) copy-start(s32[768]{0:T(1024)} %param.15) | copy-start | bytes 9220
  215.2 18.3 %collective-permute-start.4 = (f32[2,1152]{1,0:T(2,128)S(1)}, f32[2,1152]{1,0:T(2,128)S(1)}, u32[]{:S(2)}, u32[]{:S(2)}) collective-permute-start(f32[2,1152]{1,0:T(2,128)S(1)} %slice_bitcast_fusion.2), channel_id=1, source_target_pairs={{4,0},{8,4},{12,8},{16,12},{20,16},{24,20},{28,24},{5,1},{9,5},{13... | collective-permute-start | bytes 27656 | tf_op jit(solution)/shard_map/ppermute | solution.py:19
  233.6 0.6 copy-start.6
  256.9 6.0 %collective-permute-start.5 = (f32[2,2048]{1,0:T(2,128)S(1)}, f32[2,2048]{1,0:T(2,128)S(1)}, u32[]{:S(2)}, u32[]{:S(2)}) collective-permute-start(f32[2,2048]{1,0:T(2,128)S(1)} %bitcast.32), channel_id=1, source_target_pairs={{4,0},{8,4},{12,8},{16,12},{20,16},{24,20},{28,24},{5,1},{9,5},{13... | collective-permute-start | bytes 49160 | tf_op jit(solution)/shard_map/ppermute | solution.py:19
Sparse Core Ops, SparseCore 0:
  11.9 152.9 all-gather.2
